TPU v7x, 32 devices: a whole 2x2x4 slice. The times are simulated.
32 devices in a mesh: rows: 8 (over y, x, core), cols: 4 (over z).
Axes of the slice: x: 2, y: 2, z: 4, core: 2. Of those that a mesh axis runs over, the one named last changes fastest.
Arguments:
- embeddings: bfloat16 [65536, 2048], P('rows', 'cols'), may hold values from -6 to 6
- pick_rows: int32 [2, 32], replicated, may hold values from 0 to 65535, as said below
Outputs:
- residual: float32 [65536, 2048], P('rows', 'cols')
Inputs may be any that keep to these rules, and one draw needn't show every extreme that they name: `pick_rows`: all 64 indices are distinct; the picks of one round fall on the row owners as evenly as their count allows.
All inputs are finite; a program needn't handle non-finite values.
Results may differ from a plain program's by a relative error of at most 0.0003.
Values sent between devices are 32-bit elements; how exact they have to be, the bound alone decides.
A program may use at most 128 MiB of HBM per device.

v0:
```python
import jax
import jax.numpy as jnp
from jax import lax
from jax.sharding import PartitionSpec as P

HIGH = lax.Precision.HIGHEST


def orthonormal_panel(pick_panel):
    gram_matrix = jnp.dot(
        pick_panel, pick_panel.T, precision=HIGH, preferred_element_type=jnp.float32
    )
    factor = jnp.linalg.cholesky(gram_matrix)
    return jax.scipy.linalg.solve_triangular(factor, pick_panel, lower=True)


def gather_panel(residual, wanted):
    row_count, width_part = residual.shape
    first_row = lax.axis_index("rows") * row_count
    local_index = jnp.clip(wanted - first_row, 0, row_count - 1)
    owned = (wanted >= first_row) & (wanted < first_row + row_count)
    taken = jnp.take(residual, local_index, axis=0)
    partial_panel = jnp.where(owned[:, None], taken, jnp.zeros_like(taken))
    summed = lax.psum(partial_panel, "rows")
    return lax.all_gather(summed, "cols", axis=1, tiled=True)


def column_part(basis_rows, width_part):
    return lax.dynamic_slice_in_dim(basis_rows, lax.axis_index("cols") * width_part, width_part, 1)


def per_device(embeddings, pick_rows):
    residual = embeddings.astype(jnp.float32)
    width_part = residual.shape[1]
    rounds_total = pick_rows.shape[0]
    for round_index in range(rounds_total):
        pick_panel = gather_panel(residual, pick_rows[round_index])
        local_basis = column_part(orthonormal_panel(pick_panel), width_part)
        partial_weights = jnp.dot(
            residual, local_basis.T, precision=HIGH, preferred_element_type=jnp.float32
        )
        weights = lax.psum(partial_weights, "cols")
        residual = residual - jnp.dot(
            weights, local_basis, precision=HIGH, preferred_element_type=jnp.float32
        )
    return residual


def solution(mesh):
    in_specs = (P("rows", "cols"), P())
    out_specs = P("rows", "cols")
    return jax.shard_map(
        per_device, mesh=mesh, in_specs=in_specs, out_specs=out_specs, check_vma=False
    )
```

profile of v0, /device:TPU:0, one launch (start us, length us, event | category | flops | bytes accessed | tf_op | source)
XLA Modules:
  0.0 364.7 jit_solution(763248617219044473)
XLA Ops:
  6.5 0.8 compare_and_fusion
  7.3 0.8 and_bitcast_fusion
  8.1 12.0 %convert_element_type.3 = f32[8192,512]{1,0:T(8,128)} convert(bf16[8192,512]{1,0:T(8,128)(2,1)} %param.7) | non-fusion elementwise | flops 4194304 | bytes 25165824 | tf_op jit(solution)/shard_map/convert_element_type | solution.py:33
  20.0 6.4 %gather_fusion = f32[32,512]{1,0:T(8,128)S(1)} fusion(f32[8192,512]{1,0:T(8,128)} %convert_element_type.3, s32[1024]{0:T(1024)S(1)} %pad_clamp_fusion.1), kind=kCustom, calls=%fused_computation.clone | custom fusion | bytes 131200 | tf_op jit(solution)/shard_map/jit(_take)/gather | solution.py:22
  26.4 0.7 select_select_fusion.1
  27.2 55.3 %all-reduce.5.cloned.1.call-done = f32[32,512]{1,0:T(8,128)} async-done(((f32[32,512]{1,0:T(8,128)}), f32[32,512]{1,0:T(8,128)}) %all-reduce.5.cloned.1.call-update) | async-done | bytes 65552 | tf_op jit(solution)/shard_map/psum | solution.py:24
  82.5 14.1 %all_gather.6 = f32[32,2048]{1,0:T(8,128)S(1)} all-gather(f32[32,512]{1,0:T(8,128)} %all-reduce.5.cloned.1.call-done), channel_id=1, replica_groups=mesh['rows'=8,'cols'=4] {'cols'}, dimensions={1}, use_global_device_ids=true | all-gather | bytes 327680 | tf_op jit(solution)/shard_map/all_gather | solution.py:25
  97.1 2.9 cholesky.44
  100.7 0.7 fusion.5
  101.3 2.4 custom-call.6
  104.2 10.5 %convolution_bitcast_fusion = f32[8192,32]{0,1:T(8,128)} fusion(bf16[8192,512]{1,0:T(8,128)(2,1)} %param.7, f32[32,2048]{1,0:T(8,128)S(1)} %fusion.10, s32[]{:T(128)S(6)} %select_n.22), kind=kOutput, calls=%fused_computation.4 | convolution fusion | flops 1610612736 | bytes 9502724 | tf_op jit(solution)/shard_map/dot_general | solution.py:39
  114.8 51.4 %all-reduce.7.cloned.1.call-done = f32[8192,32]{0,1:T(8,128)} async-done(((f32[8192,32]{0,1:T(8,128)}), f32[8192,32]{0,1:T(8,128)}) %all-reduce.7.cloned.1.call-update) | async-done | bytes 1048592 | tf_op jit(solution)/shard_map/psum | solution.py:42
  166.3 18.6 %convolution_subtract_fusion.1 = f32[8192,512]{1,0:T(8,128)} fusion(f32[8192,32]{0,1:T(8,128)} %all-reduce.7.cloned.1.call-done, bf16[8192,512]{1,0:T(8,128)(2,1)} %param.7, f32[32,2048]{1,0:T(8,128)S(1)} %fusion.10, s32[]{:T(128)S(6)} %select_n.22), kind=kOutput, calls=%fused_computation.3 | convolution fusion | flops 1619001344 | bytes 26279940 | tf_op jit(solution)/shard_map/dot_general | solution.py:43
  184.9 6.4 %gather_fusion.1 = f32[32,512]{1,0:T(8,128)S(1)} fusion(f32[8192,512]{1,0:T(8,128)} %convolution_subtract_fusion.1, s32[1024]{0:T(1024)S(1)} %pad_clamp_fusion), kind=kCustom, calls=%fused_computation.1.clone | custom fusion | bytes 131200 | tf_op jit(solution)/shard_map/jit(_take)/gather | solution.py:22
  191.3 0.7 select_select_fusion
  192.0 51.9 %all-reduce.9.cloned.1.call-done = f32[32,512]{1,0:T(8,128)} async-done(((f32[32,512]{1,0:T(8,128)}), f32[32,512]{1,0:T(8,128)}) %all-reduce.9.cloned.1.call-update) | async-done | bytes 65552 | tf_op jit(solution)/shard_map/psum | solution.py:24
  244.0 14.3 %all_gather.7 = f32[32,2048]{1,0:T(8,128)S(1)} all-gather(f32[32,512]{1,0:T(8,128)} %all-reduce.9.cloned.1.call-done), channel_id=1, replica_groups=mesh['rows'=8,'cols'=4] {'cols'}, dimensions={1}, use_global_device_ids=true | all-gather | bytes 327680 | tf_op jit(solution)/shard_map/all_gather | solution.py:25
  258.7 2.9 cholesky.55
  261.7 0.7 compare_reduce_fusion
  262.4 0.7 fusion.6
  263.1 2.4 custom-call.7
  266.0 19.9 %fusion.1 = f32[8192,32]{0,1:T(8,128)} fusion(f32[8192,512]{1,0:T(8,128)} %convolution_subtract_fusion.1, f32[32,2048]{1,0:T(8,128)S(1)} %fusion.7, s32[]{:T(128)S(6)} %select_n.22), kind=kOutput, calls=%fused_computation.8 | convolution fusion | flops 1610612736 | bytes 17891332 | tf_op jit(solution)/shard_map/dot_general | solution.py:39
  285.9 51.5 %all-reduce.11.cloned.1.call-done = f32[8192,32]{0,1:T(8,128)} async-done(((f32[8192,32]{0,1:T(8,128)}), f32[8192,32]{0,1:T(8,128)}) %all-reduce.11.cloned.1.call-update) | async-done | bytes 1048592 | tf_op jit(solution)/shard_map/psum | solution.py:42
  337.4 20.7 %convolution_subtract_fusion = f32[8192,512]{1,0:T(8,128)} fusion(f32[8192,512]{1,0:T(8,128)} %convolution_subtract_fusion.1, f32[8192,32]{0,1:T(8,128)} %all-reduce.11.cloned.1.call-done, f32[32,2048]{1,0:T(8,128)S(1)} %fusion.7, s32[]{:T(128)S(6)} %select_n.22), kind=kOutput, calls=%fused_computation.2 | convolution fusion | flops 1614807040 | bytes 34668548 | tf_op jit(solution)/shard_map/dot_general | solution.py:43
  (21 shorter events, 2.6 us)
Async XLA Ops:
  6.5 76.0 %all-reduce.5.cloned.1.call-start = ((), (), s32[]{:S(2)}) async-start(), calls=%async_computation | async-start | bytes 131072 | tf_op jit(solution)/shard_map/psum | solution.py:24
  27.2 139.1 %all-reduce.7.cloned.1.call-start = ((), (), s32[]{:S(2)}) async-start(), calls=%async_computation.1 | async-start | bytes 2097152 | tf_op jit(solution)/shard_map/psum | solution.py:42
  114.8 129.2 %all-reduce.9.cloned.1.call-start = ((), (), s32[]{:S(2)}) async-start(), calls=%async_computation.2 | async-start | bytes 131072 | tf_op jit(solution)/shard_map/psum | solution.py:24
  192.0 145.4 %all-reduce.11.cloned.1.call-start = ((), (), s32[]{:S(2)}) async-start(), calls=%async_computation.3 | async-start | bytes 2097152 | tf_op jit(solution)/shard_map/psum | solution.py:42
Sparse Core Ops, SparseCore 0:
  27.3 55.1 all-reduce.4
  114.9 51.3 all-reduce.6
  192.1 51.8 all-reduce.8
  286.0 51.3 all-reduce.10
where the time goes:
time: 365 us
  waiting for transfers between devices  210 us (58%)
  matrix products  71.4 us (20%)
  other arithmetic  28.4 us (8%)
  blocking collectives  28.4 us (8%)
  between operations  13.2 us (4%)
  local copies, waits for them, and re-layouts  12.9 us (4%)
    psum x2, waiting for transfers between devices, gather_panel(): summed = lax.psum(partial_panel, 'rows')  107 us
    psum x2, waiting for transfers between devices, per_device(): weights = lax.psum(partial_weights, 'cols')  103 us
    dot_general x2, matrix products, per_device(): jnp.dot(weights, local_basis, precision=HIGH, preferred_element_type=jnp....  39.3 us
    dot_general x2, matrix products, per_device(): jnp.dot(residual, local_basis.T, precision=HIGH, preferred_element_type=j...  30.4 us
    all_gather x2, blocking collectives, gather_panel(): return lax.all_gather(summed, 'cols', axis=1, tiled=True)  28.4 us
    gather x2, local copies, waits for them, and re-layouts, gather_panel(): taken = jnp.take(residual, local_index, axis=0)  12.8 us
    convert_element_type x1, other arithmetic, per_device(): residual = embeddings.astype(jnp.float32)  12 us
  transfers between devices with their start and end apart: 4, of which 4 were waited for; matrix products, arithmetic and copies ran while one was open for 0% of the time, Pallas kernels for 0%

commit v1 on v0

v1 whole, which is shorter than its diff:
```python
import functools

import jax
import jax.numpy as jnp
from jax import lax
from jax.experimental import pallas as pl
from jax.experimental.pallas import tpu as pltpu
from jax.sharding import PartitionSpec as P

HIGH = lax.Precision.HIGHEST
MESH = pl.DeviceIdType.MESH
GROUP = 16
CHUNKS = 32
LAG = 2
SOLVE_STEPS = 4
VMEM_LIMIT = 56 * 1024 * 1024


def own_picks_kernel(own_count, picks_ref, first_ref, emb_ref, out_ref, groups, offsets, sems):
    row_count = emb_ref.shape[0]
    total = picks_ref.shape[0]
    first = first_ref[0]

    def look(index, found):
        local = picks_ref[index] - first
        owned = (local >= 0) & (local < row_count) & (found < own_count)

        @pl.when(owned)
        def _():
            start = pl.multiple_of((local // GROUP) * GROUP, GROUP)
            offsets[found] = local - start
            pltpu.make_async_copy(
                emb_ref.at[pl.ds(start, GROUP), :], groups.at[found], sems.at[found]
            ).start()

        return found + owned.astype(jnp.int32)

    lax.fori_loop(0, total, look, jnp.int32(0))
    for slot in range(own_count):
        pltpu.make_async_copy(
            emb_ref.at[pl.ds(0, GROUP), :], groups.at[slot], sems.at[slot]
        ).wait()
        rows = groups[slot].astype(jnp.float32)
        inside = lax.broadcasted_iota(jnp.int32, rows.shape, 0) == offsets[slot]
        out_ref[pl.ds(slot, 1), :] = jnp.sum(jnp.where(inside, rows, 0.0), axis=0, keepdims=True)


def own_picks(embeddings, picks, first, own_count):
    width = embeddings.shape[1]
    return pl.pallas_call(
        functools.partial(own_picks_kernel, own_count),
        out_shape=jax.ShapeDtypeStruct((own_count, width), jnp.float32),
        in_specs=[
            pl.BlockSpec(memory_space=pltpu.SMEM),
            pl.BlockSpec(memory_space=pltpu.SMEM),
            pl.BlockSpec(memory_space=pl.ANY),
        ],
        out_specs=pl.BlockSpec(memory_space=pltpu.VMEM),
        scratch_shapes=[
            pltpu.VMEM((own_count, GROUP, width), embeddings.dtype),
            pltpu.SMEM((own_count,), jnp.int32),
            pltpu.SemaphoreType.DMA((own_count,)),
        ],
    )(picks, first, embeddings)


def weights_kernel(
    rows_n, cols_n, chunks, emb_ref, own_ref, weights_ref, panels_ref,
    emb, gathered, panel_t, system, mine, from_left, from_right, to_right, to_left,
    emb_sem, row_send, row_recv, right_send, left_recv, left_send, right_recv,
):
    own_count, width = own_ref.shape
    rank = rows_n * own_count
    half = rank // 2
    size = weights_ref.shape[0] // chunks
    row = lax.axis_index("rows")
    col = lax.axis_index("cols")
    has_left = col > 0
    has_right = col < cols_n - 1

    load = pltpu.make_async_copy(emb_ref, emb, emb_sem)
    load.start()

    barrier = pltpu.get_barrier_semaphore()
    for step in range(1, rows_n):
        pl.semaphore_signal(
            barrier, inc=1, device_id={"rows": lax.rem(row + step, rows_n)}, device_id_type=MESH
        )

    @pl.when(has_left)
    def _():
        pl.semaphore_signal(barrier, inc=1, device_id={"cols": col - 1}, device_id_type=MESH)

    @pl.when(has_right)
    def _():
        pl.semaphore_signal(barrier, inc=1, device_id={"cols": col + 1}, device_id_type=MESH)

    @pl.when(jnp.logical_not(has_left))
    def _():
        from_left[...] = jnp.zeros_like(from_left)

    @pl.when(jnp.logical_not(has_right))
    def _():
        from_right[...] = jnp.zeros_like(from_right)

    pl.semaphore_wait(
        barrier, rows_n - 1 + has_left.astype(jnp.int32) + has_right.astype(jnp.int32)
    )

    def row_copy(step):
        return pltpu.make_async_remote_copy(
            src_ref=own_ref,
            dst_ref=gathered.at[row],
            send_sem=row_send.at[step],
            recv_sem=row_recv.at[row],
            device_id={"rows": lax.rem(row + step, rows_n)},
            device_id_type=MESH,
        )

    for step in range(1, rows_n):
        row_copy(step).start()
    gathered[row] = own_ref[...]
    mine[pl.ds(0, size), :] = jnp.zeros((size, 2 * rank), jnp.float32)
    for step in range(1, rows_n):
        source = lax.rem(row + step, rows_n)
        pltpu.make_async_remote_copy(
            src_ref=own_ref,
            dst_ref=gathered.at[source],
            send_sem=row_send.at[step],
            recv_sem=row_recv.at[source],
            device_id={"rows": source},
            device_id_type=MESH,
        ).wait_recv()

    panel = jnp.concatenate([gathered[owner] for owner in range(rows_n)], axis=0)
    panel16 = panel.astype(jnp.bfloat16)
    nothing = jnp.zeros_like(panel)
    for side in range(2):
        padded = jnp.concatenate([panel, nothing] if side == 0 else [nothing, panel], axis=0)
        panel_t[side] = padded.T.astype(jnp.bfloat16)
        for piece in range(3):
            panels_ref[side, pl.ds(piece * 2 * rank, 2 * rank), :] = padded.astype(jnp.bfloat16)

    mine[pl.ds(0, half), :] = jnp.dot(
        panel16[:half], panel_t[0], preferred_element_type=jnp.float32
    ) + jnp.dot(panel16[half:], panel_t[1], preferred_element_type=jnp.float32)

    def part(index):
        return pl.ds(pl.multiple_of(index * size, size), size)

    def right_copy(index):
        return pltpu.make_async_remote_copy(
            src_ref=to_right.at[part(index)],
            dst_ref=from_left.at[part(index)],
            send_sem=right_send.at[index],
            recv_sem=left_recv.at[index],
            device_id={"cols": lax.rem(col + 1, cols_n)},
            device_id_type=MESH,
        )

    def left_copy(index):
        return pltpu.make_async_remote_copy(
            src_ref=to_left.at[part(index)],
            dst_ref=from_right.at[part(index)],
            send_sem=left_send.at[index],
            recv_sem=right_recv.at[index],
            device_id={"cols": lax.rem(col + cols_n - 1, cols_n)},
            device_id_type=MESH,
        )

    parts = chunks + 1
    hops = (cols_n - 1) * LAG
    solve_from = hops + 1
    solve_turns = rank // SOLVE_STEPS
    weigh_from = solve_from + solve_turns
    turns = parts + hops
    lanes = lax.broadcasted_iota(jnp.int32, (rank, 2 * rank), 1)
    sublanes = lax.broadcasted_iota(jnp.int32, (rank, 2 * rank), 0)
    load.wait()

    def summed(index):
        return mine[part(index), :] + from_left[part(index), :] + from_right[part(index), :]

    def eliminate(step, _):
        now = system[0:rank, :]
        picked = system[pl.ds(step, 1), :]
        on_lane = lanes == step
        on_row = sublanes == step
        column = jnp.sum(jnp.where(on_lane, now, 0.0), axis=1, keepdims=True)
        pivot = jnp.sum(jnp.where(on_lane[0:1], picked, 0.0), axis=1, keepdims=True)
        new_row = jnp.where(on_lane[0:1], 1.0, picked) / pivot
        rest = jnp.where(on_lane, 0.0, now) - column * new_row
        system[0:rank, :] = jnp.where(on_row, jnp.broadcast_to(new_row, now.shape), rest)
        return 0

    def weigh(index):
        at = pl.ds(pl.multiple_of((index - 1) * size, size), size)
        weights_ref[at, :] = jnp.dot(
            summed(index), system[...], precision=HIGH, preferred_element_type=jnp.float32
        )

    def turn(index, _):
        @pl.when((index >= 1) & (index < parts))
        def _():
            at = pl.ds(pl.multiple_of((index - 1) * size, size), size)
            mine[part(index), :] = jnp.dot(
                emb[0, at, :], panel_t[0], preferred_element_type=jnp.float32
            ) + jnp.dot(emb[1, at, :], panel_t[1], preferred_element_type=jnp.float32)

        left_index = index - col * LAG
        right_index = index - (cols_n - 1 - col) * LAG

        @pl.when((left_index >= 0) & (left_index < parts))
        def _():
            @pl.when(has_left)
            def _():
                right_copy(left_index).wait_recv()

            @pl.when(has_right)
            def _():
                to_right[part(left_index), :] = (
                    mine[part(left_index), :] + from_left[part(left_index), :]
                )
                right_copy(left_index).start()

        @pl.when((right_index >= 0) & (right_index < parts))
        def _():
            @pl.when(has_right)
            def _():
                left_copy(right_index).wait_recv()

            @pl.when(has_left)
            def _():
                to_left[part(right_index), :] = (
                    mine[part(right_index), :] + from_right[part(right_index), :]
                )
                left_copy(right_index).start()

        @pl.when(index == hops)
        def _():
            at = pl.ds(0, half)
            packed = mine[at, :] + from_left[at, :] + from_right[at, :]
            inside = lanes[0:half] < rank
            system[0:half, :] = jnp.where(inside, packed, 0.0)
            system[half:rank, :] = jnp.where(inside, pltpu.roll(packed, rank, 1), 0.0)

        @pl.when((index >= solve_from) & (index < weigh_from))
        def _():
            lax.fori_loop(
                (index - solve_from) * SOLVE_STEPS,
                (index - solve_from + 1) * SOLVE_STEPS,
                eliminate,
                0,
            )

        @pl.when(index == weigh_from)
        def _():
            system[rank : 2 * rank, :] = pltpu.roll(system[0:rank, :], rank, 1)

        @pl.when(index >= weigh_from)
        def _():
            weigh((index - weigh_from) * 2 + 1)
            weigh((index - weigh_from) * 2 + 2)

        return 0

    lax.fori_loop(0, turns, turn, 0)
    weighed = (turns - weigh_from) * 2

    def finish(index, _):
        weigh(index)
        return 0

    lax.fori_loop(weighed + 1, parts, finish, 0)

    for step in range(1, rows_n):
        row_copy(step).wait_send()

    def sent(index, _):
        @pl.when(has_right)
        def _():
            right_copy(index).wait_send()

        @pl.when(has_left)
        def _():
            left_copy(index).wait_send()

        return 0

    lax.fori_loop(0, parts, sent, 0)


def all_weights(emb3, own, rows_n, cols_n, rank):
    _, pairs, width = emb3.shape
    size = pairs // CHUNKS
    buffer = pltpu.VMEM((pairs + size, 2 * rank), jnp.float32)
    dma = pltpu.SemaphoreType.DMA
    return pl.pallas_call(
        functools.partial(weights_kernel, rows_n, cols_n, CHUNKS),
        out_shape=(
            jax.ShapeDtypeStruct((pairs, 2 * rank), jnp.float32),
            jax.ShapeDtypeStruct((2, 6 * rank, width), jnp.bfloat16),
        ),
        in_specs=[pl.BlockSpec(memory_space=pl.ANY), pl.BlockSpec(memory_space=pltpu.VMEM)],
        out_specs=(
            pl.BlockSpec(memory_space=pltpu.VMEM),
            pl.BlockSpec(memory_space=pltpu.VMEM),
        ),
        scratch_shapes=[
            pltpu.VMEM(emb3.shape, emb3.dtype),
            pltpu.VMEM((rows_n,) + own.shape, jnp.float32),
            pltpu.VMEM((2, width, 2 * rank), jnp.bfloat16),
            pltpu.VMEM((2 * rank, 2 * rank), jnp.float32),
            buffer, buffer, buffer, buffer, buffer,
            dma, dma((rows_n,)), dma((rows_n,)),
            dma((CHUNKS + 1,)), dma((CHUNKS + 1,)), dma((CHUNKS + 1,)), dma((CHUNKS + 1,)),
        ],
        compiler_params=pltpu.CompilerParams(
            collective_id=0, has_side_effects=True, vmem_limit_bytes=VMEM_LIMIT
        ),
        cost_estimate=pl.CostEstimate(
            flops=8 * pairs * width * rank, bytes_accessed=2 * emb3.size, transcendentals=0
        ),
    )(emb3, own)


def subtract_kernel(emb_ref, weights_ref, panels_ref, out_ref):
    weights = weights_ref[...]
    first = weights.astype(jnp.bfloat16)
    rest = weights - first.astype(jnp.float32)
    second = rest.astype(jnp.bfloat16)
    third = (rest - second.astype(jnp.float32)).astype(jnp.bfloat16)
    pieces = jnp.concatenate([first, second, third], axis=1)
    for side in range(2):
        out_ref[side] = emb_ref[side].astype(jnp.float32) - jnp.dot(
            pieces, panels_ref[side], preferred_element_type=jnp.float32
        )


def subtract(emb3, weights, panels):
    _, pairs, width = emb3.shape
    block = min(512, pairs)
    return pl.pallas_call(
        subtract_kernel,
        grid=(pairs // block,),
        out_shape=jax.ShapeDtypeStruct(emb3.shape, jnp.float32),
        in_specs=[
            pl.BlockSpec((2, block, width), lambda i: (0, i, 0)),
            pl.BlockSpec((block, weights.shape[1]), lambda i: (i, 0)),
            pl.BlockSpec(panels.shape, lambda i: (0, 0, 0)),
        ],
        out_specs=pl.BlockSpec((2, block, width), lambda i: (0, i, 0)),
        compiler_params=pltpu.CompilerParams(vmem_limit_bytes=VMEM_LIMIT),
    )(emb3, weights, panels)


def per_device(rows_n, cols_n, embeddings, pick_rows):
    row_count, width = embeddings.shape
    rank = pick_rows.shape[0] * pick_rows.shape[1]
    first = (lax.axis_index("rows") * row_count).astype(jnp.int32).reshape(1)
    own = own_picks(embeddings, pick_rows.reshape(rank), first, rank // rows_n)
    emb3 = embeddings.reshape(2, row_count // 2, width)
    weights, panels = all_weights(emb3, own, rows_n, cols_n, rank)
    return subtract(emb3, weights, panels).reshape(row_count, width)


def solution(mesh):
    in_specs = (P("rows", "cols"), P())
    out_specs = P("rows", "cols")
    return jax.shard_map(
        functools.partial(per_device, mesh.shape["rows"], mesh.shape["cols"]),
        mesh=mesh, in_specs=in_specs, out_specs=out_specs, check_vma=False,
    )
```

time: 365 us -> 95.5 us (0.26)
  waiting for transfers between devices: 210 us -> 0 us
  Pallas kernels: 0 us -> 93.6 us
  matrix products: 71.4 us -> 0 us
  other arithmetic: 28.4 us -> 0 us
  blocking collectives: 28.4 us -> 0 us
  between operations: 13.2 us -> 0.02 us
  local copies, waits for them, and re-layouts: 12.9 us -> 1.26 us
    psum x4 -> x0, waiting for transfers between devices: 210 us -> none  [the longest x2 107 us: gather_panel(): summed = lax.psum(partial_panel, 'rows')]
    pallas_call x0 -> x3, Pallas kernels: none -> 93.6 us  [the longest x1 77.1 us: all_weights(): pl.pallas_call(functools.partial(weights_kernel, rows_n, cols_n, CHUNKS),...]
    dot_general x6 -> x0, matrix products: 70.5 us -> none  [the longest x2 39.3 us: per_device(): jnp.dot(weights, local_basis, precision=HIGH, preferred_element_type=jnp....]
    all_gather x2 -> x0, blocking collectives: 28.4 us -> none  [gather_panel(): return lax.all_gather(summed, 'cols', axis=1, tiled=True)]
    another operation x10 -> x0, other arithmetic: 13.5 us -> none  [the longest x6 7.27 us: orthonormal_panel(): factor = jnp.linalg.cholesky(gram_matrix)]
    gather x2 -> x0, local copies, waits for them, and re-layouts: 12.8 us -> none  [gather_panel(): taken = jnp.take(residual, local_index, axis=0)]
    convert_element_type x1 -> x0, other arithmetic: 12 us -> none  [per_device(): residual = embeddings.astype(jnp.float32)]
  transfers between devices with their start and end apart: 4 -> 0, of which waited for: 4 -> 0; matrix products, arithmetic and copies ran while one was open for 0% -> 0% of each run, Pallas kernels for 0% -> 0%
where the time goes in v1:
time: 95.5 us; the launch traced here: 94.9 us
  Pallas kernels  93.6 us (98%)
  local copies, waits for them, and re-layouts  1.26 us (1%)
    pallas_call x1, Pallas kernels, all_weights(): pl.pallas_call(functools.partial(weights_kernel, rows_n, cols_n, CHUNKS),...  77.1 us
    pallas_call x1, Pallas kernels, subtract(): pl.pallas_call(subtract_kernel, grid=(pairs // block,), out_shape=jax.Sha...  13.6 us
    pallas_call x1, Pallas kernels, own_picks(): pl.pallas_call(functools.partial(own_picks_kernel, own_count), out_shape=...  2.91 us

profile of v1, /device:TPU:0, one launch (start us, length us, event | category | flops | bytes accessed | tf_op | source)
XLA Modules:
  0.0 94.9 jit_solution(200925078904253360)
XLA Ops:
  0.0 1.3 %reshape.13.picks_ref = s32[64]{0:T(128)} reshape(s32[2,32]{1,0:T(2,128)} %param.3) | data formatting | bytes 512 | tf_op jit(solution)/shard_map/reshape | solution.py:361
  1.3 2.9 %shard_map.28.own_ref = f32[8,512]{1,0:T(8,128)} custom-call(s32[64]{0:T(128)} %reshape.13.picks_ref, s32[1]{0:T(128)} %bitcast.1.first_ref, bf16[8192,512]{1,0:T(8,128)(2,1)} %emb_ref.1), custom_call_target="tpu_custom_call" | custom-call | tf_op jit(solution)/shard_map/pallas_call | solution.py:50
  4.2 77.1 %shard_map.29 = (f32[4096,128]{1,0:T(8,128)}, bf16[2,384,512]{2,1,0:T(8,128)(2,1)}) custom-call(bf16[2,4096,512]{2,1,0:T(8,128)(2,1)} %bitcast.3, f32[8,512]{1,0:T(8,128)} %shard_map.28.own_ref), custom_call_target="tpu_custom_call" | custom-call | flops 1073741824 | bytes 8388608 | tf_op jit(solution)/shard_map/pallas_call | solution.py:298
  81.3 13.6 %shard_map.30 = f32[2,4096,512]{2,1,0:T(8,128)} custom-call(bf16[2,4096,512]{2,1,0:T(8,128)(2,1)} %bitcast.4, f32[4096,128]{1,0:T(8,128)} %get-tuple-element.7.weights_ref, bf16[2,384,512]{2,1,0:T(8,128)(2,1)} %get-tuple-element.8.panels_ref), custom_call_target="tpu_custom_call" | custom-call | tf_op jit(solution)/shard_map/pallas_call | solution.py:343

commit v2 on v1

--- a/solution.py
+++ b/solution.py
@@ -11,18 +11,19 @@
 MESH = pl.DeviceIdType.MESH
 GROUP = 16
 CHUNKS = 32
-LAG = 2
+LAG = 4
+BLOCK_PARTS = 4
 SOLVE_STEPS = 4
-VMEM_LIMIT = 56 * 1024 * 1024
-
-
-def own_picks_kernel(own_count, picks_ref, first_ref, emb_ref, out_ref, groups, offsets, sems):
+MIB = 1024 * 1024
+
+
+def own_picks_kernel(own_count, picks_ref, emb_ref, out_ref, groups, offsets, sems):
     row_count = emb_ref.shape[0]
-    total = picks_ref.shape[0]
-    first = first_ref[0]
+    rounds, per_round = picks_ref.shape
+    first = lax.axis_index("rows") * row_count
 
     def look(index, found):
-        local = picks_ref[index] - first
+        local = picks_ref[index // per_round, index % per_round] - first
         owned = (local >= 0) & (local < row_count) & (found < own_count)
 
         @pl.when(owned)
@@ -35,7 +36,7 @@
 
         return found + owned.astype(jnp.int32)
 
-    lax.fori_loop(0, total, look, jnp.int32(0))
+    lax.fori_loop(0, rounds * per_round, look, jnp.int32(0), unroll=8)
     for slot in range(own_count):
         pltpu.make_async_copy(
             emb_ref.at[pl.ds(0, GROUP), :], groups.at[slot], sems.at[slot]
@@ -45,13 +46,12 @@
         out_ref[pl.ds(slot, 1), :] = jnp.sum(jnp.where(inside, rows, 0.0), axis=0, keepdims=True)
 
 
-def own_picks(embeddings, picks, first, own_count):
+def own_picks(embeddings, picks, own_count):
     width = embeddings.shape[1]
     return pl.pallas_call(
         functools.partial(own_picks_kernel, own_count),
         out_shape=jax.ShapeDtypeStruct((own_count, width), jnp.float32),
         in_specs=[
-            pl.BlockSpec(memory_space=pltpu.SMEM),
             pl.BlockSpec(memory_space=pltpu.SMEM),
             pl.BlockSpec(memory_space=pl.ANY),
         ],
@@ -61,7 +61,8 @@
             pltpu.SMEM((own_count,), jnp.int32),
             pltpu.SemaphoreType.DMA((own_count,)),
         ],
-    )(picks, first, embeddings)
+        compiler_params=pltpu.CompilerParams(vmem_limit_bytes=60 * MIB),
+    )(picks, embeddings)
 
 
 def weights_kernel(
@@ -174,12 +175,10 @@
     solve_turns = rank // SOLVE_STEPS
     weigh_from = solve_from + solve_turns
     turns = parts + hops
+    assert turns + 1 - 2 * (chunks // BLOCK_PARTS) >= weigh_from
     lanes = lax.broadcasted_iota(jnp.int32, (rank, 2 * rank), 1)
     sublanes = lax.broadcasted_iota(jnp.int32, (rank, 2 * rank), 0)
     load.wait()
-
-    def summed(index):
-        return mine[part(index), :] + from_left[part(index), :] + from_right[part(index), :]
 
     def eliminate(step, _):
         now = system[0:rank, :]
@@ -193,19 +192,32 @@
         system[0:rank, :] = jnp.where(on_row, jnp.broadcast_to(new_row, now.shape), rest)
         return 0
 
+    block = BLOCK_PARTS * size
+    blocks = chunks // BLOCK_PARTS
+
+    def block_rows(index):
+        start = pl.multiple_of(index * block, block)
+        return pl.ds(start, block), pl.ds(pl.multiple_of(start + size, size), block)
+
+    def multiply(index):
+        at, kept = block_rows(index)
+        mine[kept, :] = jnp.dot(
+            emb[0, at, :], panel_t[0], preferred_element_type=jnp.float32
+        ) + jnp.dot(emb[1, at, :], panel_t[1], preferred_element_type=jnp.float32)
+
     def weigh(index):
-        at = pl.ds(pl.multiple_of((index - 1) * size, size), size)
+        at, kept = block_rows(index)
+        total = mine[kept, :] + from_left[kept, :] + from_right[kept, :]
         weights_ref[at, :] = jnp.dot(
-            summed(index), system[...], precision=HIGH, preferred_element_type=jnp.float32
-        )
+            total, system[...], precision=HIGH, preferred_element_type=jnp.float32
+        )
+
+    multiply(0)
 
     def turn(index, _):
-        @pl.when((index >= 1) & (index < parts))
-        def _():
-            at = pl.ds(pl.multiple_of((index - 1) * size, size), size)
-            mine[part(index), :] = jnp.dot(
-                emb[0, at, :], panel_t[0], preferred_element_type=jnp.float32
-            ) + jnp.dot(emb[1, at, :], panel_t[1], preferred_element_type=jnp.float32)
+        @pl.when((index % BLOCK_PARTS == 1) & (index < chunks - BLOCK_PARTS))
+        def _():
+            multiply(index // BLOCK_PARTS + 1)
 
         left_index = index - col * LAG
         right_index = index - (cols_n - 1 - col) * LAG
@@ -257,21 +269,15 @@
         def _():
             system[rank : 2 * rank, :] = pltpu.roll(system[0:rank, :], rank, 1)
 
-        @pl.when(index >= weigh_from)
-        def _():
-            weigh((index - weigh_from) * 2 + 1)
-            weigh((index - weigh_from) * 2 + 2)
+        since = index - (turns + 1 - 2 * blocks)
+
+        @pl.when((since >= 0) & (since % 2 == 0))
+        def _():
+            weigh(since // 2)
 
         return 0
 
     lax.fori_loop(0, turns, turn, 0)
-    weighed = (turns - weigh_from) * 2
-
-    def finish(index, _):
-        weigh(index)
-        return 0
-
-    lax.fori_loop(weighed + 1, parts, finish, 0)
 
     for step in range(1, rows_n):
         row_copy(step).wait_send()
@@ -316,7 +322,7 @@
             dma((CHUNKS + 1,)), dma((CHUNKS + 1,)), dma((CHUNKS + 1,)), dma((CHUNKS + 1,)),
         ],
         compiler_params=pltpu.CompilerParams(
-            collective_id=0, has_side_effects=True, vmem_limit_bytes=VMEM_LIMIT
+            collective_id=0, has_side_effects=True, vmem_limit_bytes=28 * MIB
         ),
         cost_estimate=pl.CostEstimate(
             flops=8 * pairs * width * rank, bytes_accessed=2 * emb3.size, transcendentals=0
@@ -350,15 +356,14 @@
             pl.BlockSpec(panels.shape, lambda i: (0, 0, 0)),
         ],
         out_specs=pl.BlockSpec((2, block, width), lambda i: (0, i, 0)),
-        compiler_params=pltpu.CompilerParams(vmem_limit_bytes=VMEM_LIMIT),
+        compiler_params=pltpu.CompilerParams(vmem_limit_bytes=16 * MIB),
     )(emb3, weights, panels)
 
 
 def per_device(rows_n, cols_n, embeddings, pick_rows):
     row_count, width = embeddings.shape
     rank = pick_rows.shape[0] * pick_rows.shape[1]
-    first = (lax.axis_index("rows") * row_count).astype(jnp.int32).reshape(1)
-    own = own_picks(embeddings, pick_rows.reshape(rank), first, rank // rows_n)
+    own = own_picks(embeddings, pick_rows, rank // rows_n)
     emb3 = embeddings.reshape(2, row_count // 2, width)
     weights, panels = all_weights(emb3, own, rows_n, cols_n, rank)
     return subtract(emb3, weights, panels).reshape(row_count, width)

time: 95.5 us -> 84.9 us (0.89)
  Pallas kernels: 93.6 us -> 80.5 us
  local copies, waits for them, and re-layouts: 1.26 us -> 4.09 us
    pallas_call x1, Pallas kernels: 77.1 us -> 68.2 us  [all_weights(): pl.pallas_call(functools.partial(weights_kernel, rows_n, cols_n, CHUNKS),...]
    pallas_call x1, Pallas kernels: 13.6 us -> 9.22 us  [subtract(): pl.pallas_call(subtract_kernel, grid=(pairs // block,), out_shape=jax.Sha...]
    unnamed x0 -> x4, local copies, waits for them, and re-layouts: none -> 4.09 us
    reshape x1 -> x0, local copies, waits for them, and re-layouts: 1.26 us -> none  [per_device(): own = own_picks(embeddings, pick_rows.reshape(rank), first, rank // rows_n)]
where the time goes in v2:
time: 84.9 us; the launch traced here: 84.6 us
  Pallas kernels  80.5 us (95%)
  local copies, waits for them, and re-layouts  4.09 us (5%)
    pallas_call x1, Pallas kernels, all_weights(): pl.pallas_call(functools.partial(weights_kernel, rows_n, cols_n, CHUNKS),...  68.2 us
    pallas_call x1, Pallas kernels, subtract(): pl.pallas_call(subtract_kernel, grid=(pairs // block,), out_shape=jax.Sha...  9.22 us
    unnamed x4, local copies, waits for them, and re-layouts  4.09 us
    pallas_call x1, Pallas kernels, own_picks(): pl.pallas_call(functools.partial(own_picks_kernel, own_count), out_shape=...  3.1 us

profile of v2, /device:TPU:0, one launch (start us, length us, event | category | flops | bytes accessed | tf_op | source)
XLA Modules:
  0.0 84.6 jit_solution(13653343282942043171)
XLA Ops:
  0.0 3.1 %shard_map.28.own_ref = f32[8,512]{1,0:T(8,128)} custom-call(s32[2,32]{1,0:T(2,128)} %picks_ref.1, bf16[8192,512]{1,0:T(8,128)(2,1)} %emb_ref.1), custom_call_target="tpu_custom_call" | custom-call | tf_op jit(solution)/shard_map/pallas_call | solution.py:51
  3.1 0.0 copy-start
  3.1 3.4 %copy-done = bf16[8192,512]{1,0:T(8,128)(2,1)S(1)} copy-done((bf16[8192,512]{1,0:T(8,128)(2,1)S(1)}, bf16[8192,512]{1,0:T(8,128)(2,1)}, u32[]{:S(2)}) %copy-start) | copy-done | bytes 8388632
  6.5 0.0 copy-start.1
  6.5 0.7 copy-done.1
  7.2 68.2 %shard_map.29 = (f32[4096,128]{1,0:T(8,128)S(1)}, bf16[2,384,512]{2,1,0:T(8,128)(2,1)S(1)}) custom-call(bf16[2,4096,512]{2,1,0:T(8,128)(2,1)S(1)} %bitcast.2, f32[8,512]{1,0:T(8,128)S(1)} %copy-done.1), custom_call_target="tpu_custom_call" | custom-call | flops 1073741824 | bytes 8388608 | tf_op jit(solution)/shard_map/pallas_call | solution.py:304
  75.4 9.2 %shard_map.30 = f32[2,4096,512]{2,1,0:T(8,128)} custom-call(bf16[2,4096,512]{2,1,0:T(8,128)(2,1)S(1)} %bitcast.3, f32[4096,128]{1,0:T(8,128)S(1)} %get-tuple-element.7.weights_ref, bf16[2,384,512]{2,1,0:T(8,128)(2,1)S(1)} %get-tuple-element.8.panels_ref), custom_call_target="tpu_custom_call" | custom-call | tf_op jit(solution)/shard_map/pallas_call | solution.py:349
Async XLA Ops:
  3.1 3.4 %copy-start = (bf16[8192,512]{1,0:T(8,128)(2,1)S(1)}, bf16[8192,512]{1,0:T(8,128)(2,1)}, u32[]{:S(2)}) copy-start(bf16[8192,512]{1,0:T(8,128)(2,1)} %emb_ref.1) | copy-start | bytes 25165828
  6.5 0.7 copy-start.1

commit v3 on v2

--- a/solution.py
+++ b/solution.py
@@ -61,13 +61,13 @@
             pltpu.SMEM((own_count,), jnp.int32),
             pltpu.SemaphoreType.DMA((own_count,)),
         ],
-        compiler_params=pltpu.CompilerParams(vmem_limit_bytes=60 * MIB),
+        compiler_params=pltpu.CompilerParams(vmem_limit_bytes=52 * MIB),
     )(picks, embeddings)
 
 
 def weights_kernel(
-    rows_n, cols_n, chunks, emb_ref, own_ref, weights_ref, panels_ref,
-    emb, gathered, panel_t, system, mine, from_left, from_right, to_right, to_left,
+    rows_n, cols_n, chunks, emb_ref, own_ref, emb, weights_ref, panels_ref,
+    gathered, panel_t, system, mine, from_left, from_right, to_right, to_left,
     emb_sem, row_send, row_recv, right_send, left_recv, left_send, right_recv,
 ):
     own_count, width = own_ref.shape
@@ -121,7 +121,6 @@
     for step in range(1, rows_n):
         row_copy(step).start()
     gathered[row] = own_ref[...]
-    mine[pl.ds(0, size), :] = jnp.zeros((size, 2 * rank), jnp.float32)
     for step in range(1, rows_n):
         source = lax.rem(row + step, rows_n)
         pltpu.make_async_remote_copy(
@@ -133,14 +132,14 @@
             device_id_type=MESH,
         ).wait_recv()
 
-    panel = jnp.concatenate([gathered[owner] for owner in range(rows_n)], axis=0)
-    panel16 = panel.astype(jnp.bfloat16)
-    nothing = jnp.zeros_like(panel)
+    def padded_panel(side):
+        panel = jnp.concatenate([gathered[owner] for owner in range(rows_n)], axis=0)
+        nothing = jnp.zeros_like(panel)
+        return jnp.concatenate([panel, nothing] if side == 0 else [nothing, panel], axis=0)
+
     for side in range(2):
-        padded = jnp.concatenate([panel, nothing] if side == 0 else [nothing, panel], axis=0)
-        panel_t[side] = padded.T.astype(jnp.bfloat16)
-        for piece in range(3):
-            panels_ref[side, pl.ds(piece * 2 * rank, 2 * rank), :] = padded.astype(jnp.bfloat16)
+        panel_t[side] = padded_panel(side).T.astype(jnp.bfloat16)
+    panel16 = padded_panel(0)[:rank].astype(jnp.bfloat16)
 
     mine[pl.ds(0, half), :] = jnp.dot(
         panel16[:half], panel_t[0], preferred_element_type=jnp.float32
@@ -149,20 +148,20 @@
     def part(index):
         return pl.ds(pl.multiple_of(index * size, size), size)
 
-    def right_copy(index):
+    def right_copy(index, at):
         return pltpu.make_async_remote_copy(
-            src_ref=to_right.at[part(index)],
-            dst_ref=from_left.at[part(index)],
+            src_ref=to_right.at[at],
+            dst_ref=from_left.at[at],
             send_sem=right_send.at[index],
             recv_sem=left_recv.at[index],
             device_id={"cols": lax.rem(col + 1, cols_n)},
             device_id_type=MESH,
         )
 
-    def left_copy(index):
+    def left_copy(index, at):
         return pltpu.make_async_remote_copy(
-            src_ref=to_left.at[part(index)],
-            dst_ref=from_right.at[part(index)],
+            src_ref=to_left.at[at],
+            dst_ref=from_right.at[at],
             send_sem=left_send.at[index],
             recv_sem=right_recv.at[index],
             device_id={"cols": lax.rem(col + cols_n - 1, cols_n)},
@@ -178,7 +177,6 @@
     assert turns + 1 - 2 * (chunks // BLOCK_PARTS) >= weigh_from
     lanes = lax.broadcasted_iota(jnp.int32, (rank, 2 * rank), 1)
     sublanes = lax.broadcasted_iota(jnp.int32, (rank, 2 * rank), 0)
-    load.wait()
 
     def eliminate(step, _):
         now = system[0:rank, :]
@@ -200,6 +198,10 @@
         return pl.ds(start, block), pl.ds(pl.multiple_of(start + size, size), block)
 
     def multiply(index):
+        @pl.when(index == 0)
+        def _():
+            load.wait()
+
         at, kept = block_rows(index)
         mine[kept, :] = jnp.dot(
             emb[0, at, :], panel_t[0], preferred_element_type=jnp.float32
@@ -212,41 +214,58 @@
             total, system[...], precision=HIGH, preferred_element_type=jnp.float32
         )
 
-    multiply(0)
+    gram_at = pl.ds(0, half)
+
+    def pass_right(index, at):
+        @pl.when(has_left)
+        def _():
+            right_copy(index, at).wait_recv()
+
+        @pl.when(has_right)
+        def _():
+            to_right[at, :] = mine[at, :] + from_left[at, :]
+            right_copy(index, at).start()
+
+    def pass_left(index, at):
+        @pl.when(has_right)
+        def _():
+            left_copy(index, at).wait_recv()
+
+        @pl.when(has_left)
+        def _():
+            to_left[at, :] = mine[at, :] + from_right[at, :]
+            left_copy(index, at).start()
 
     def turn(index, _):
-        @pl.when((index % BLOCK_PARTS == 1) & (index < chunks - BLOCK_PARTS))
-        def _():
-            multiply(index // BLOCK_PARTS + 1)
-
         left_index = index - col * LAG
         right_index = index - (cols_n - 1 - col) * LAG
 
-        @pl.when((left_index >= 0) & (left_index < parts))
-        def _():
-            @pl.when(has_left)
-            def _():
-                right_copy(left_index).wait_recv()
-
-            @pl.when(has_right)
-            def _():
-                to_right[part(left_index), :] = (
-                    mine[part(left_index), :] + from_left[part(left_index), :]
-                )
-                right_copy(left_index).start()
-
-        @pl.when((right_index >= 0) & (right_index < parts))
-        def _():
-            @pl.when(has_right)
-            def _():
-                left_copy(right_index).wait_recv()
-
-            @pl.when(has_left)
-            def _():
-                to_left[part(right_index), :] = (
-                    mine[part(right_index), :] + from_right[part(right_index), :]
-                )
-                left_copy(right_index).start()
+        @pl.when(left_index == 0)
+        def _():
+            pass_right(left_index, gram_at)
+
+        @pl.when((left_index >= 1) & (left_index < parts))
+        def _():
+            pass_right(left_index, part(left_index))
+
+        @pl.when(right_index == 0)
+        def _():
+            pass_left(right_index, gram_at)
+
+        @pl.when((right_index >= 1) & (right_index < parts))
+        def _():
+            pass_left(right_index, part(right_index))
+
+        @pl.when((index % BLOCK_PARTS == 0) & (index < chunks))
+        def _():
+            multiply(index // BLOCK_PARTS)
+
+        @pl.when(index == 2)
+        def _():
+            for side in range(2):
+                padded = padded_panel(side).astype(jnp.bfloat16)
+                for piece in range(3):
+                    panels_ref[side, pl.ds(piece * 2 * rank, 2 * rank), :] = padded
 
         @pl.when(index == hops)
         def _():
@@ -282,18 +301,21 @@
     for step in range(1, rows_n):
         row_copy(step).wait_send()
 
+    def wait_sent(index, at):
+        @pl.when(has_right)
+        def _():
+            right_copy(index, at).wait_send()
+
+        @pl.when(has_left)
+        def _():
+            left_copy(index, at).wait_send()
+
     def sent(index, _):
-        @pl.when(has_right)
-        def _():
-            right_copy(index).wait_send()
-
-        @pl.when(has_left)
-        def _():
-            left_copy(index).wait_send()
-
+        wait_sent(index, part(index))
         return 0
 
-    lax.fori_loop(0, parts, sent, 0)
+    wait_sent(0, gram_at)
+    lax.fori_loop(1, parts, sent, 0)
 
 
 def all_weights(emb3, own, rows_n, cols_n, rank):
@@ -304,16 +326,13 @@
     return pl.pallas_call(
         functools.partial(weights_kernel, rows_n, cols_n, CHUNKS),
         out_shape=(
+            jax.ShapeDtypeStruct(emb3.shape, emb3.dtype),
             jax.ShapeDtypeStruct((pairs, 2 * rank), jnp.float32),
             jax.ShapeDtypeStruct((2, 6 * rank, width), jnp.bfloat16),
         ),
         in_specs=[pl.BlockSpec(memory_space=pl.ANY), pl.BlockSpec(memory_space=pltpu.VMEM)],
-        out_specs=(
-            pl.BlockSpec(memory_space=pltpu.VMEM),
-            pl.BlockSpec(memory_space=pltpu.VMEM),
-        ),
+        out_specs=(pl.BlockSpec(memory_space=pltpu.VMEM),) * 3,
         scratch_shapes=[
-            pltpu.VMEM(emb3.shape, emb3.dtype),
             pltpu.VMEM((rows_n,) + own.shape, jnp.float32),
             pltpu.VMEM((2, width, 2 * rank), jnp.bfloat16),
             pltpu.VMEM((2 * rank, 2 * rank), jnp.float32),
@@ -322,7 +341,7 @@
             dma((CHUNKS + 1,)), dma((CHUNKS + 1,)), dma((CHUNKS + 1,)), dma((CHUNKS + 1,)),
         ],
         compiler_params=pltpu.CompilerParams(
-            collective_id=0, has_side_effects=True, vmem_limit_bytes=28 * MIB
+            collective_id=0, has_side_effects=True, vmem_limit_bytes=40 * MIB
         ),
         cost_estimate=pl.CostEstimate(
             flops=8 * pairs * width * rank, bytes_accessed=2 * emb3.size, transcendentals=0
@@ -345,7 +364,7 @@
 
 def subtract(emb3, weights, panels):
     _, pairs, width = emb3.shape
-    block = min(512, pairs)
+    block = min(256, pairs)
     return pl.pallas_call(
         subtract_kernel,
         grid=(pairs // block,),
@@ -365,8 +384,8 @@
     rank = pick_rows.shape[0] * pick_rows.shape[1]
     own = own_picks(embeddings, pick_rows, rank // rows_n)
     emb3 = embeddings.reshape(2, row_count // 2, width)
-    weights, panels = all_weights(emb3, own, rows_n, cols_n, rank)
-    return subtract(emb3, weights, panels).reshape(row_count, width)
+    held, weights, panels = all_weights(emb3, own, rows_n, cols_n, rank)
+    return subtract(held, weights, panels).reshape(row_count, width)
 
 
 def solution(mesh):

time: 84.9 us -> 81.7 us (0.962)
  local copies, waits for them, and re-layouts: 4.09 us -> 0.68 us
    unnamed x4 -> x2, local copies, waits for them, and re-layouts: 4.09 us -> 0.68 us
    pallas_call x1, Pallas kernels: 9.22 us -> 12 us  [subtract(): pl.pallas_call(subtract_kernel, grid=(pairs // block,), out_shape=jax.Sha...]
    pallas_call x1, Pallas kernels: 68.2 us -> 66.4 us  [all_weights(): pl.pallas_call(functools.partial(weights_kernel, rows_n, cols_n, CHUNKS),...]
where the time goes in v3:
time: 81.7 us; the launch traced here: 81.5 us
  Pallas kernels  80.8 us (99%)
    pallas_call x1, Pallas kernels, all_weights(): pl.pallas_call(functools.partial(weights_kernel, rows_n, cols_n, CHUNKS),...  66.4 us
    pallas_call x1, Pallas kernels, subtract(): pl.pallas_call(subtract_kernel, grid=(pairs // block,), out_shape=jax.Sha...  12 us
    pallas_call x1, Pallas kernels, own_picks(): pl.pallas_call(functools.partial(own_picks_kernel, own_count), out_shape=...  2.41 us

profile of v3, /device:TPU:0, one launch (start us, length us, event | category | flops | bytes accessed | tf_op | source)
XLA Modules:
  0.0 81.5 jit_solution(18052539263661748513)
XLA Ops:
  0.0 0.0 copy-start
  0.0 0.7 copy-done
  0.7 2.4 %shard_map.28.own_ref = f32[8,512]{1,0:T(8,128)S(1)} custom-call(s32[2,32]{1,0:T(2,128)S(1)} %copy-done, bf16[8192,512]{1,0:T(8,128)(2,1)} %emb_ref.1), custom_call_target="tpu_custom_call" | custom-call | tf_op jit(solution)/shard_map/pallas_call | solution.py:51
  3.1 66.4 %shard_map.29 = (bf16[2,4096,512]{2,1,0:T(8,128)(2,1)S(1)}, f32[4096,128]{1,0:T(8,128)S(1)}, bf16[2,384,512]{2,1,0:T(8,128)(2,1)S(1)}) custom-call(bf16[2,4096,512]{2,1,0:T(8,128)(2,1)} %bitcast.2, f32[8,512]{1,0:T(8,128)S(1)} %shard_map.28.own_ref), custom_call_target="tpu_custom_call" | custom-call | flops 1073741824 | bytes 8388608 | tf_op jit(solution)/shard_map/pallas_call | solution.py:326
  69.5 12.0 %shard_map.30 = f32[2,4096,512]{2,1,0:T(8,128)} custom-call(bf16[2,4096,512]{2,1,0:T(8,128)(2,1)S(1)} %get-tuple-element.8.emb_ref, f32[4096,128]{1,0:T(8,128)S(1)} %get-tuple-element.9.weights_ref, bf16[2,384,512]{2,1,0:T(8,128)(2,1)S(1)} %get-tuple-element.10.panels_ref), custom_call_target="tpu_custom_call" | custom-call | tf_op jit(solution)/shard_map/pallas_call | solution.py:368
Async XLA Ops:
  0.0 0.7 copy-start

commit v4 on v3

--- a/solution.py
+++ b/solution.py
@@ -13,6 +13,7 @@
 CHUNKS = 32
 LAG = 4
 BLOCK_PARTS = 4
+EARLY_BLOCKS = 6
 SOLVE_STEPS = 4
 MIB = 1024 * 1024
 
@@ -65,10 +66,19 @@
     )(picks, embeddings)
 
 
+def residual_rows(emb, weights, panel):
+    first = weights.astype(jnp.bfloat16)
+    rest = weights - first.astype(jnp.float32)
+    second = rest.astype(jnp.bfloat16)
+    third = (rest - second.astype(jnp.float32)).astype(jnp.bfloat16)
+    pieces = jnp.concatenate([first, second, third], axis=1)
+    return emb.astype(jnp.float32) - jnp.dot(pieces, panel, preferred_element_type=jnp.float32)
+
+
 def weights_kernel(
-    rows_n, cols_n, chunks, emb_ref, own_ref, emb, weights_ref, panels_ref,
+    rows_n, cols_n, chunks, emb, own_ref, weights_ref, panels_ref, early_ref,
     gathered, panel_t, system, mine, from_left, from_right, to_right, to_left,
-    emb_sem, row_send, row_recv, right_send, left_recv, left_send, right_recv,
+    row_send, row_recv, right_send, left_recv, left_send, right_recv,
 ):
     own_count, width = own_ref.shape
     rank = rows_n * own_count
@@ -78,9 +88,6 @@
     col = lax.axis_index("cols")
     has_left = col > 0
     has_right = col < cols_n - 1
-
-    load = pltpu.make_async_copy(emb_ref, emb, emb_sem)
-    load.start()
 
     barrier = pltpu.get_barrier_semaphore()
     for step in range(1, rows_n):
@@ -198,10 +205,6 @@
         return pl.ds(start, block), pl.ds(pl.multiple_of(start + size, size), block)
 
     def multiply(index):
-        @pl.when(index == 0)
-        def _():
-            load.wait()
-
         at, kept = block_rows(index)
         mine[kept, :] = jnp.dot(
             emb[0, at, :], panel_t[0], preferred_element_type=jnp.float32
@@ -289,6 +292,14 @@
             system[rank : 2 * rank, :] = pltpu.roll(system[0:rank, :], rank, 1)
 
         since = index - (turns + 1 - 2 * blocks)
+
+        @pl.when((since >= 0) & (since % 2 == 1) & (since < 2 * EARLY_BLOCKS))
+        def _():
+            at, _ = block_rows(since // 2)
+            for side in range(2):
+                early_ref[side, at, :] = residual_rows(
+                    emb[side, at, :], weights_ref[at, :], panels_ref[side]
+                )
 
         @pl.when((since >= 0) & (since % 2 == 0))
         def _():
@@ -326,22 +337,22 @@
     return pl.pallas_call(
         functools.partial(weights_kernel, rows_n, cols_n, CHUNKS),
         out_shape=(
-            jax.ShapeDtypeStruct(emb3.shape, emb3.dtype),
             jax.ShapeDtypeStruct((pairs, 2 * rank), jnp.float32),
             jax.ShapeDtypeStruct((2, 6 * rank, width), jnp.bfloat16),
+            jax.ShapeDtypeStruct((2, EARLY_BLOCKS * BLOCK_PARTS * size, width), jnp.float32),
         ),
-        in_specs=[pl.BlockSpec(memory_space=pl.ANY), pl.BlockSpec(memory_space=pltpu.VMEM)],
+        in_specs=[pl.BlockSpec(memory_space=pltpu.VMEM)] * 2,
         out_specs=(pl.BlockSpec(memory_space=pltpu.VMEM),) * 3,
         scratch_shapes=[
             pltpu.VMEM((rows_n,) + own.shape, jnp.float32),
             pltpu.VMEM((2, width, 2 * rank), jnp.bfloat16),
             pltpu.VMEM((2 * rank, 2 * rank), jnp.float32),
             buffer, buffer, buffer, buffer, buffer,
-            dma, dma((rows_n,)), dma((rows_n,)),
+            dma((rows_n,)), dma((rows_n,)),
             dma((CHUNKS + 1,)), dma((CHUNKS + 1,)), dma((CHUNKS + 1,)), dma((CHUNKS + 1,)),
         ],
         compiler_params=pltpu.CompilerParams(
-            collective_id=0, has_side_effects=True, vmem_limit_bytes=40 * MIB
+            collective_id=0, has_side_effects=True, vmem_limit_bytes=24 * MIB
         ),
         cost_estimate=pl.CostEstimate(
             flops=8 * pairs * width * rank, bytes_accessed=2 * emb3.size, transcendentals=0
@@ -349,34 +360,61 @@
     )(emb3, own)
 
 
-def subtract_kernel(emb_ref, weights_ref, panels_ref, out_ref):
-    weights = weights_ref[...]
-    first = weights.astype(jnp.bfloat16)
-    rest = weights - first.astype(jnp.float32)
-    second = rest.astype(jnp.bfloat16)
-    third = (rest - second.astype(jnp.float32)).astype(jnp.bfloat16)
-    pieces = jnp.concatenate([first, second, third], axis=1)
-    for side in range(2):
-        out_ref[side] = emb_ref[side].astype(jnp.float32) - jnp.dot(
-            pieces, panels_ref[side], preferred_element_type=jnp.float32
-        )
-
-
-def subtract(emb3, weights, panels):
+def last_kernel(
+    block, emb_ref, weights_ref, panels_ref, early_ref, out_ref,
+    emb, late, emb_sem, early_sems, late_sems,
+):
+    early = early_ref.shape[1] // block
+    late_count = late.shape[1] // block
+    load = pltpu.make_async_copy(emb_ref.at[:, pl.ds(early * block, late_count * block), :], emb, emb_sem)
+    load.start()
+    copies = []
+    for index in range(early):
+        at = pl.ds(index * block, block)
+        for side in range(2):
+            copies.append(
+                pltpu.make_async_copy(
+                    early_ref.at[side, at], out_ref.at[side, at], early_sems.at[index, side]
+                )
+            )
+            copies[-1].start()
+    load.wait()
+    for index in range(late_count):
+        here = pl.ds(index * block, block)
+        at = pl.ds((early + index) * block, block)
+        for side in range(2):
+            late[side, here, :] = residual_rows(
+                emb[side, here, :], weights_ref[at, :], panels_ref[side]
+            )
+            copies.append(
+                pltpu.make_async_copy(
+                    late.at[side, here], out_ref.at[side, at], late_sems.at[index, side]
+                )
+            )
+            copies[-1].start()
+    for copy in copies:
+        copy.wait()
+
+
+def last_rows(emb3, weights, panels, early):
     _, pairs, width = emb3.shape
-    block = min(256, pairs)
+    block = BLOCK_PARTS * (pairs // CHUNKS)
+    late = pairs - early.shape[1]
+    dma = pltpu.SemaphoreType.DMA
+    anywhere = pl.BlockSpec(memory_space=pl.ANY)
+    inside = pl.BlockSpec(memory_space=pltpu.VMEM)
     return pl.pallas_call(
-        subtract_kernel,
-        grid=(pairs // block,),
+        functools.partial(last_kernel, block),
         out_shape=jax.ShapeDtypeStruct(emb3.shape, jnp.float32),
-        in_specs=[
-            pl.BlockSpec((2, block, width), lambda i: (0, i, 0)),
-            pl.BlockSpec((block, weights.shape[1]), lambda i: (i, 0)),
-            pl.BlockSpec(panels.shape, lambda i: (0, 0, 0)),
+        in_specs=[anywhere, inside, inside, anywhere],
+        out_specs=anywhere,
+        scratch_shapes=[
+            pltpu.VMEM((2, late, width), emb3.dtype),
+            pltpu.VMEM((2, late, width), jnp.float32),
+            dma, dma((early.shape[1] // block, 2)), dma((late // block, 2)),
         ],
-        out_specs=pl.BlockSpec((2, block, width), lambda i: (0, i, 0)),
-        compiler_params=pltpu.CompilerParams(vmem_limit_bytes=16 * MIB),
-    )(emb3, weights, panels)
+        compiler_params=pltpu.CompilerParams(vmem_limit_bytes=24 * MIB),
+    )(emb3, weights, panels, early)
 
 
 def per_device(rows_n, cols_n, embeddings, pick_rows):
@@ -384,8 +422,8 @@
     rank = pick_rows.shape[0] * pick_rows.shape[1]
     own = own_picks(embeddings, pick_rows, rank // rows_n)
     emb3 = embeddings.reshape(2, row_count // 2, width)
-    held, weights, panels = all_weights(emb3, own, rows_n, cols_n, rank)
-    return subtract(held, weights, panels).reshape(row_count, width)
+    parts = all_weights(emb3, own, rows_n, cols_n, rank)
+    return last_rows(emb3, *parts).reshape(row_count, width)
 
 
 def solution(mesh):

time: 81.7 us -> 76.2 us (0.933)
  Pallas kernels: 80.8 us -> 74.8 us
    pallas_call x1, Pallas kernels: 12 us -> 6.11 us  [last_rows(): pl.pallas_call(functools.partial(last_kernel, block), out_shape=jax.Shape...]
where the time goes in v4:
time: 76.2 us; the launch traced here: 75.9 us
  Pallas kernels  74.8 us (98%)
  local copies, waits for them, and re-layouts  1.05 us (1%)
    pallas_call x1, Pallas kernels, all_weights(): pl.pallas_call(functools.partial(weights_kernel, rows_n, cols_n, CHUNKS),...  66.3 us
    pallas_call x1, Pallas kernels, last_rows(): pl.pallas_call(functools.partial(last_kernel, block), out_shape=jax.Shape...  6.11 us
    pallas_call x1, Pallas kernels, own_picks(): pl.pallas_call(functools.partial(own_picks_kernel, own_count), out_shape=...  2.46 us

profile of v4, /device:TPU:0, one launch (start us, length us, event | category | flops | bytes accessed | tf_op | source)
XLA Modules:
  0.0 75.9 jit_solution(15930127334133080697)
XLA Ops:
  0.0 0.0 copy-start
  0.0 0.0 copy-start.1
  0.0 0.8 %copy-done.1 = s32[2,32]{1,0:T(2,128)S(1)} copy-done((s32[2,32]{1,0:T(2,128)S(1)}, s32[2,32]{1,0:T(2,128)}, u32[]{:S(2)}) %copy-start.1) | copy-done | bytes 280
  0.8 2.5 %shard_map.28.own_ref = f32[8,512]{1,0:T(8,128)S(1)} custom-call(s32[2,32]{1,0:T(2,128)S(1)} %copy-done.1, bf16[8192,512]{1,0:T(8,128)(2,1)} %emb_ref.1), custom_call_target="tpu_custom_call" | custom-call | tf_op jit(solution)/shard_map/pallas_call | solution.py:52
  3.3 0.2 copy-done
  3.5 66.3 %shard_map.29 = (f32[4096,128]{1,0:T(8,128)S(1)}, bf16[2,384,512]{2,1,0:T(8,128)(2,1)S(1)}, f32[2,3072,512]{2,1,0:T(8,128)S(1)}) custom-call(bf16[2,4096,512]{2,1,0:T(8,128)(2,1)S(1)} %bitcast.2, f32[8,512]{1,0:T(8,128)S(1)} %shard_map.28.own_ref), custom_call_target="tpu_custom_call" | custom-call | flops 1073741824 | bytes 8388608 | tf_op jit(solution)/shard_map/pallas_call | solution.py:337
  69.8 6.1 %shard_map.30 = f32[2,4096,512]{2,1,0:T(8,128)} custom-call(bf16[2,4096,512]{2,1,0:T(8,128)(2,1)S(1)} %bitcast.3, f32[4096,128]{1,0:T(8,128)S(1)} %get-tuple-element.8.weights_ref, bf16[2,384,512]{2,1,0:T(8,128)(2,1)S(1)} %get-tuple-element.9.panels_ref, f32[2,3072,512]{2,1,0:T(8,128)S(1)} %get-tuple-element.10.early_ref), custom_call_target="tpu_custom_call" | custom-call | tf_op jit(solution)/shard_map/pallas_call | solution.py:406
Async XLA Ops:
  0.0 3.5 %copy-start = (bf16[8192,512]{1,0:T(8,128)(2,1)S(1)}, bf16[8192,512]{1,0:T(8,128)(2,1)}, u32[]{:S(2)}) copy-start(bf16[8192,512]{1,0:T(8,128)(2,1)} %emb_ref.1) | copy-start | bytes 25165828
  0.0 0.8 %copy-start.1 = (s32[2,32]{1,0:T(2,128)S(1)}, s32[2,32]{1,0:T(2,128)}, u32[]{:S(2)}) copy-start(s32[2,32]{1,0:T(2,128)} %picks_ref.1) | copy-start | bytes 772

commit v5 on v4

--- a/solution.py
+++ b/solution.py
@@ -10,11 +10,12 @@
 HIGH = lax.Precision.HIGHEST
 MESH = pl.DeviceIdType.MESH
 GROUP = 16
-CHUNKS = 32
-LAG = 4
-BLOCK_PARTS = 4
+CHUNKS = 64
+LAG = 8
+BLOCK_PARTS = 8
+STRIDE = 4
 EARLY_BLOCKS = 6
-SOLVE_STEPS = 4
+SOLVE_STEPS = 2
 MIB = 1024 * 1024
 
 
@@ -76,8 +77,8 @@
 
 
 def weights_kernel(
-    rows_n, cols_n, chunks, emb, own_ref, weights_ref, panels_ref, early_ref,
-    gathered, panel_t, system, mine, from_left, from_right, to_right, to_left,
+    rows_n, cols_n, chunks, emb, own_ref, weights_ref, panels_ref, early_ref, system,
+    gathered, panel_t, mine, from_left, from_right, to_right, to_left,
     row_send, row_recv, right_send, left_recv, left_send, right_recv,
 ):
     own_count, width = own_ref.shape
@@ -159,7 +160,7 @@
         return pltpu.make_async_remote_copy(
             src_ref=to_right.at[at],
             dst_ref=from_left.at[at],
-            send_sem=right_send.at[index],
+            send_sem=right_send,
             recv_sem=left_recv.at[index],
             device_id={"cols": lax.rem(col + 1, cols_n)},
             device_id_type=MESH,
@@ -169,7 +170,7 @@
         return pltpu.make_async_remote_copy(
             src_ref=to_left.at[at],
             dst_ref=from_right.at[at],
-            send_sem=left_send.at[index],
+            send_sem=left_send,
             recv_sem=right_recv.at[index],
             device_id={"cols": lax.rem(col + cols_n - 1, cols_n)},
             device_id_type=MESH,
@@ -181,7 +182,7 @@
     solve_turns = rank // SOLVE_STEPS
     weigh_from = solve_from + solve_turns
     turns = parts + hops
-    assert turns + 1 - 2 * (chunks // BLOCK_PARTS) >= weigh_from
+    assert turns - 1 - STRIDE * (chunks // BLOCK_PARTS - 1) >= weigh_from
     lanes = lax.broadcasted_iota(jnp.int32, (rank, 2 * rank), 1)
     sublanes = lax.broadcasted_iota(jnp.int32, (rank, 2 * rank), 0)
 
@@ -210,11 +211,13 @@
             emb[0, at, :], panel_t[0], preferred_element_type=jnp.float32
         ) + jnp.dot(emb[1, at, :], panel_t[1], preferred_element_type=jnp.float32)
 
+    def block_sum(kept):
+        return mine[kept, :] + from_left[kept, :] + from_right[kept, :]
+
     def weigh(index):
         at, kept = block_rows(index)
-        total = mine[kept, :] + from_left[kept, :] + from_right[kept, :]
         weights_ref[at, :] = jnp.dot(
-            total, system[...], precision=HIGH, preferred_element_type=jnp.float32
+            block_sum(kept), system[...], precision=HIGH, preferred_element_type=jnp.float32
         )
 
     gram_at = pl.ds(0, half)
@@ -291,23 +294,25 @@
         def _():
             system[rank : 2 * rank, :] = pltpu.roll(system[0:rank, :], rank, 1)
 
-        since = index - (turns + 1 - 2 * blocks)
-
-        @pl.when((since >= 0) & (since % 2 == 1) & (since < 2 * EARLY_BLOCKS))
-        def _():
-            at, _ = block_rows(since // 2)
+        since = index - (turns - 1 - STRIDE * (blocks - 1))
+
+        @pl.when((since >= 0) & (since % STRIDE == STRIDE // 2) & (since < STRIDE * EARLY_BLOCKS))
+        def _():
+            at, _ = block_rows(since // STRIDE)
             for side in range(2):
                 early_ref[side, at, :] = residual_rows(
                     emb[side, at, :], weights_ref[at, :], panels_ref[side]
                 )
 
-        @pl.when((since >= 0) & (since % 2 == 0))
-        def _():
-            weigh(since // 2)
+        @pl.when((since >= 0) & (since % STRIDE == 0) & (since < STRIDE * (blocks - 1)))
+        def _():
+            weigh(since // STRIDE)
 
         return 0
 
     lax.fori_loop(0, turns, turn, 0)
+    at, kept = block_rows(blocks - 1)
+    weights_ref[at, :] = block_sum(kept)
 
     for step in range(1, rows_n):
         row_copy(step).wait_send()
@@ -321,12 +326,7 @@
         def _():
             left_copy(index, at).wait_send()
 
-    def sent(index, _):
-        wait_sent(index, part(index))
-        return 0
-
-    wait_sent(0, gram_at)
-    lax.fori_loop(1, parts, sent, 0)
+    wait_sent(0, pl.ds(size - half, chunks * size + half))
 
 
 def all_weights(emb3, own, rows_n, cols_n, rank):
@@ -340,19 +340,19 @@
             jax.ShapeDtypeStruct((pairs, 2 * rank), jnp.float32),
             jax.ShapeDtypeStruct((2, 6 * rank, width), jnp.bfloat16),
             jax.ShapeDtypeStruct((2, EARLY_BLOCKS * BLOCK_PARTS * size, width), jnp.float32),
+            jax.ShapeDtypeStruct((2 * rank, 2 * rank), jnp.float32),
         ),
         in_specs=[pl.BlockSpec(memory_space=pltpu.VMEM)] * 2,
-        out_specs=(pl.BlockSpec(memory_space=pltpu.VMEM),) * 3,
+        out_specs=(pl.BlockSpec(memory_space=pltpu.VMEM),) * 4,
         scratch_shapes=[
             pltpu.VMEM((rows_n,) + own.shape, jnp.float32),
             pltpu.VMEM((2, width, 2 * rank), jnp.bfloat16),
-            pltpu.VMEM((2 * rank, 2 * rank), jnp.float32),
             buffer, buffer, buffer, buffer, buffer,
             dma((rows_n,)), dma((rows_n,)),
-            dma((CHUNKS + 1,)), dma((CHUNKS + 1,)), dma((CHUNKS + 1,)), dma((CHUNKS + 1,)),
+            dma, dma((CHUNKS + 1,)), dma, dma((CHUNKS + 1,)),
         ],
         compiler_params=pltpu.CompilerParams(
-            collective_id=0, has_side_effects=True, vmem_limit_bytes=24 * MIB
+            collective_id=0, has_side_effects=True, vmem_limit_bytes=16 * MIB
         ),
         cost_estimate=pl.CostEstimate(
             flops=8 * pairs * width * rank, bytes_accessed=2 * emb3.size, transcendentals=0
@@ -361,7 +361,7 @@
 
 
 def last_kernel(
-    block, emb_ref, weights_ref, panels_ref, early_ref, out_ref,
+    block, emb_ref, weights_ref, panels_ref, early_ref, system_ref, out_ref,
     emb, late, emb_sem, early_sems, late_sems,
 ):
     early = early_ref.shape[1] // block
@@ -382,10 +382,13 @@
     for index in range(late_count):
         here = pl.ds(index * block, block)
         at = pl.ds((early + index) * block, block)
+        weights = weights_ref[at, :]
+        if index == late_count - 1:
+            weights = jnp.dot(
+                weights, system_ref[...], precision=HIGH, preferred_element_type=jnp.float32
+            )
         for side in range(2):
-            late[side, here, :] = residual_rows(
-                emb[side, here, :], weights_ref[at, :], panels_ref[side]
-            )
+            late[side, here, :] = residual_rows(emb[side, here, :], weights, panels_ref[side])
             copies.append(
                 pltpu.make_async_copy(
                     late.at[side, here], out_ref.at[side, at], late_sems.at[index, side]
@@ -396,7 +399,7 @@
         copy.wait()
 
 
-def last_rows(emb3, weights, panels, early):
+def last_rows(emb3, weights, panels, early, system):
     _, pairs, width = emb3.shape
     block = BLOCK_PARTS * (pairs // CHUNKS)
     late = pairs - early.shape[1]
@@ -406,15 +409,15 @@
     return pl.pallas_call(
         functools.partial(last_kernel, block),
         out_shape=jax.ShapeDtypeStruct(emb3.shape, jnp.float32),
-        in_specs=[anywhere, inside, inside, anywhere],
+        in_specs=[anywhere, inside, inside, anywhere, inside],
         out_specs=anywhere,
         scratch_shapes=[
             pltpu.VMEM((2, late, width), emb3.dtype),
             pltpu.VMEM((2, late, width), jnp.float32),
             dma, dma((early.shape[1] // block, 2)), dma((late // block, 2)),
         ],
-        compiler_params=pltpu.CompilerParams(vmem_limit_bytes=24 * MIB),
-    )(emb3, weights, panels, early)
+        compiler_params=pltpu.CompilerParams(vmem_limit_bytes=12 * MIB),
+    )(emb3, weights, panels, early, system)
 
 
 def per_device(rows_n, cols_n, embeddings, pick_rows):

time: 76.2 us -> 75 us (0.984)
  Pallas kernels: 74.8 us -> 73.7 us
    pallas_call x1, Pallas kernels: 66.3 us -> 65.1 us  [all_weights(): pl.pallas_call(functools.partial(weights_kernel, rows_n, cols_n, CHUNKS),...]
where the time goes in v5:
time: 75 us; the launch traced here: 74.8 us
  Pallas kernels  73.7 us (98%)
  local copies, waits for them, and re-layouts  1.05 us (1%)
    pallas_call x1, Pallas kernels, all_weights(): pl.pallas_call(functools.partial(weights_kernel, rows_n, cols_n, CHUNKS),...  65.1 us
    pallas_call x1, Pallas kernels, last_rows(): pl.pallas_call(functools.partial(last_kernel, block), out_shape=jax.Shape...  6.11 us
    pallas_call x1, Pallas kernels, own_picks(): pl.pallas_call(functools.partial(own_picks_kernel, own_count), out_shape=...  2.46 us

profile of v5, /device:TPU:0, one launch (start us, length us, event | category | flops | bytes accessed | tf_op | source)
XLA Modules:
  0.0 74.8 jit_solution(7524527652617091396)
XLA Ops:
  0.0 0.0 copy-start
  0.0 0.0 copy-start.1
  0.0 0.8 %copy-done.1 = s32[2,32]{1,0:T(2,128)S(1)} copy-done((s32[2,32]{1,0:T(2,128)S(1)}, s32[2,32]{1,0:T(2,128)}, u32[]{:S(2)}) %copy-start.1) | copy-done | bytes 280
  0.8 2.5 %shard_map.28.own_ref = f32[8,512]{1,0:T(8,128)S(1)} custom-call(s32[2,32]{1,0:T(2,128)S(1)} %copy-done.1, bf16[8192,512]{1,0:T(8,128)(2,1)} %emb_ref.1), custom_call_target="tpu_custom_call" | custom-call | tf_op jit(solution)/shard_map/pallas_call | solution.py:53
  3.3 0.2 copy-done
  3.5 65.1 %shard_map.29 = (f32[4096,128]{1,0:T(8,128)S(1)}, bf16[2,384,512]{2,1,0:T(8,128)(2,1)S(1)}, f32[2,3072,512]{2,1,0:T(8,128)S(1)}, f32[128,128]{1,0:T(8,128)S(1)}) custom-call(bf16[2,4096,512]{2,1,0:T(8,128)(2,1)S(1)} %bitcast.2, f32[8,512]{1,0:T(8,128)S(1)} %shard_map.28.own_ref), custom_call_target="tpu_custom_call" | custom-call | flops 1073741824 | bytes 8388608 | tf_op jit(solution)/shard_map/pallas_call | solution.py:337
  68.7 6.1 %shard_map.30 = f32[2,4096,512]{2,1,0:T(8,128)} custom-call(bf16[2,4096,512]{2,1,0:T(8,128)(2,1)S(1)} %bitcast.3, f32[4096,128]{1,0:T(8,128)S(1)} %get-tuple-element.9.weights_ref, bf16[2,384,512]{2,1,0:T(8,128)(2,1)S(1)} %get-tuple-element.10.panels_ref, f32[2,3072,512]{2,1,0:T(8,128)S(1)} %get-tuple-element.11.early_ref, ...), custom_call_target="tpu_custom_call" | custom-call | tf_op jit(solution)/shard_map/pallas_call | solution.py:409
Async XLA Ops:
  0.0 3.5 %copy-start = (bf16[8192,512]{1,0:T(8,128)(2,1)S(1)}, bf16[8192,512]{1,0:T(8,128)(2,1)}, u32[]{:S(2)}) copy-start(bf16[8192,512]{1,0:T(8,128)(2,1)} %emb_ref.1) | copy-start | bytes 25165828
  0.0 0.8 %copy-start.1 = (s32[2,32]{1,0:T(2,128)S(1)}, s32[2,32]{1,0:T(2,128)}, u32[]{:S(2)}) copy-start(s32[2,32]{1,0:T(2,128)} %picks_ref.1) | copy-start | bytes 772

commit v6 on v5

--- a/solution.py
+++ b/solution.py
@@ -11,10 +11,11 @@
 MESH = pl.DeviceIdType.MESH
 GROUP = 16
 CHUNKS = 64
-LAG = 8
+LAG = 6
 BLOCK_PARTS = 8
 STRIDE = 4
-EARLY_BLOCKS = 6
+EARLY_BLOCKS = 5
+LATE_WEIGHED = 2
 SOLVE_STEPS = 2
 MIB = 1024 * 1024
 
@@ -304,15 +305,16 @@
                     emb[side, at, :], weights_ref[at, :], panels_ref[side]
                 )
 
-        @pl.when((since >= 0) & (since % STRIDE == 0) & (since < STRIDE * (blocks - 1)))
+        @pl.when((since >= 0) & (since % STRIDE == 0) & (since < STRIDE * (blocks - LATE_WEIGHED)))
         def _():
             weigh(since // STRIDE)
 
         return 0
 
     lax.fori_loop(0, turns, turn, 0)
-    at, kept = block_rows(blocks - 1)
-    weights_ref[at, :] = block_sum(kept)
+    for index in range(blocks - LATE_WEIGHED, blocks):
+        at, kept = block_rows(index)
+        weights_ref[at, :] = block_sum(kept)
 
     for step in range(1, rows_n):
         row_copy(step).wait_send()
@@ -383,7 +385,7 @@
         here = pl.ds(index * block, block)
         at = pl.ds((early + index) * block, block)
         weights = weights_ref[at, :]
-        if index == late_count - 1:
+        if index >= late_count - LATE_WEIGHED:
             weights = jnp.dot(
                 weights, system_ref[...], precision=HIGH, preferred_element_type=jnp.float32
             )
@@ -416,7 +418,7 @@
             pltpu.VMEM((2, late, width), jnp.float32),
             dma, dma((early.shape[1] // block, 2)), dma((late // block, 2)),
         ],
-        compiler_params=pltpu.CompilerParams(vmem_limit_bytes=12 * MIB),
+        compiler_params=pltpu.CompilerParams(vmem_limit_bytes=16 * MIB),
     )(emb3, weights, panels, early, system)
 
 

time: 75 us -> 74 us (0.987)
  Pallas kernels: 73.7 us -> 72.6 us
    pallas_call x1, Pallas kernels: 65.1 us -> 64 us  [all_weights(): pl.pallas_call(functools.partial(weights_kernel, rows_n, cols_n, CHUNKS),...]
where the time goes in v6:
time: 74 us; the launch traced here: 73.7 us
  Pallas kernels  72.6 us (98%)
  local copies, waits for them, and re-layouts  1.12 us (2%)
    pallas_call x1, Pallas kernels, all_weights(): pl.pallas_call(functools.partial(weights_kernel, rows_n, cols_n, CHUNKS),...  64 us
    pallas_call x1, Pallas kernels, last_rows(): pl.pallas_call(functools.partial(last_kernel, block), out_shape=jax.Shape...  6.18 us
    pallas_call x1, Pallas kernels, own_picks(): pl.pallas_call(functools.partial(own_picks_kernel, own_count), out_shape=...  2.4 us

profile of v6, /device:TPU:0, one launch (start us, length us, event | category | flops | bytes accessed | tf_op | source)
XLA Modules:
  0.0 73.7 jit_solution(14798458746758776338)
XLA Ops:
  0.0 0.0 copy-start
  0.0 0.0 copy-start.1
  0.0 0.8 %copy-done.1 = s32[2,32]{1,0:T(2,128)S(1)} copy-done((s32[2,32]{1,0:T(2,128)S(1)}, s32[2,32]{1,0:T(2,128)}, u32[]{:S(2)}) %copy-start.1) | copy-done | bytes 280
  0.8 2.4 %shard_map.28.own_ref = f32[8,512]{1,0:T(8,128)S(1)} custom-call(s32[2,32]{1,0:T(2,128)S(1)} %copy-done.1, bf16[8192,512]{1,0:T(8,128)(2,1)} %emb_ref.1), custom_call_target="tpu_custom_call" | custom-call | tf_op jit(solution)/shard_map/pallas_call | solution.py:54
  3.2 0.3 copy-done
  3.5 64.0 %shard_map.29 = (f32[4096,128]{1,0:T(8,128)S(1)}, bf16[2,384,512]{2,1,0:T(8,128)(2,1)S(1)}, f32[2,2560,512]{2,1,0:T(8,128)S(1)}, f32[128,128]{1,0:T(8,128)S(1)}) custom-call(bf16[2,4096,512]{2,1,0:T(8,128)(2,1)S(1)} %bitcast.2, f32[8,512]{1,0:T(8,128)S(1)} %shard_map.28.own_ref), custom_call_target="tpu_custom_call" | custom-call | flops 1073741824 | bytes 8388608 | tf_op jit(solution)/shard_map/pallas_call | solution.py:339
  67.6 6.2 %shard_map.30 = f32[2,4096,512]{2,1,0:T(8,128)} custom-call(bf16[2,4096,512]{2,1,0:T(8,128)(2,1)S(1)} %bitcast.3, f32[4096,128]{1,0:T(8,128)S(1)} %get-tuple-element.9.weights_ref, bf16[2,384,512]{2,1,0:T(8,128)(2,1)S(1)} %get-tuple-element.10.panels_ref, f32[2,2560,512]{2,1,0:T(8,128)S(1)} %get-tuple-element.11.early_ref, ...), custom_call_target="tpu_custom_call" | custom-call | tf_op jit(solution)/shard_map/pallas_call | solution.py:411
Async XLA Ops:
  0.0 3.5 %copy-start = (bf16[8192,512]{1,0:T(8,128)(2,1)S(1)}, bf16[8192,512]{1,0:T(8,128)(2,1)}, u32[]{:S(2)}) copy-start(bf16[8192,512]{1,0:T(8,128)(2,1)} %emb_ref.1) | copy-start | bytes 25165828
  0.0 0.8 %copy-start.1 = (s32[2,32]{1,0:T(2,128)S(1)}, s32[2,32]{1,0:T(2,128)}, u32[]{:S(2)}) copy-start(s32[2,32]{1,0:T(2,128)} %picks_ref.1) | copy-start | bytes 772

commit v7 on v6

--- a/solution.py
+++ b/solution.py
@@ -10,13 +10,13 @@
 HIGH = lax.Precision.HIGHEST
 MESH = pl.DeviceIdType.MESH
 GROUP = 16
-CHUNKS = 64
-LAG = 6
-BLOCK_PARTS = 8
-STRIDE = 4
+CHUNKS = 32
+LAG = 3
+BLOCK_PARTS = 4
+STRIDE = 2
 EARLY_BLOCKS = 5
 LATE_WEIGHED = 2
-SOLVE_STEPS = 2
+SOLVE_STEPS = 4
 MIB = 1024 * 1024
 
 

time: 74 us -> 74.2 us (level)
  no operation moved by 1% of the time
where the time goes in v7:
time: 74.2 us; the launch traced here: 74 us
  Pallas kernels  72.9 us (98%)
  local copies, waits for them, and re-layouts  1.07 us (1%)
    pallas_call x1, Pallas kernels, all_weights(): pl.pallas_call(functools.partial(weights_kernel, rows_n, cols_n, CHUNKS),...  64.3 us
    pallas_call x1, Pallas kernels, last_rows(): pl.pallas_call(functools.partial(last_kernel, block), out_shape=jax.Shape...  6.18 us
    pallas_call x1, Pallas kernels, own_picks(): pl.pallas_call(functools.partial(own_picks_kernel, own_count), out_shape=...  2.44 us

profile of v7, /device:TPU:0, one launch (start us, length us, event | category | flops | bytes accessed | tf_op | source)
XLA Modules:
  0.0 74.0 jit_solution(12263676268749414732)
XLA Ops:
  0.0 0.0 copy-start
  0.0 0.0 copy-start.1
  0.0 0.8 %copy-done.1 = s32[2,32]{1,0:T(2,128)S(1)} copy-done((s32[2,32]{1,0:T(2,128)S(1)}, s32[2,32]{1,0:T(2,128)}, u32[]{:S(2)}) %copy-start.1) | copy-done | bytes 280
  0.8 2.4 %shard_map.28.own_ref = f32[8,512]{1,0:T(8,128)S(1)} custom-call(s32[2,32]{1,0:T(2,128)S(1)} %copy-done.1, bf16[8192,512]{1,0:T(8,128)(2,1)} %emb_ref.1), custom_call_target="tpu_custom_call" | custom-call | tf_op jit(solution)/shard_map/pallas_call | solution.py:54
  3.3 0.2 copy-done
  3.5 64.3 %shard_map.29 = (f32[4096,128]{1,0:T(8,128)S(1)}, bf16[2,384,512]{2,1,0:T(8,128)(2,1)S(1)}, f32[2,2560,512]{2,1,0:T(8,128)S(1)}, f32[128,128]{1,0:T(8,128)S(1)}) custom-call(bf16[2,4096,512]{2,1,0:T(8,128)(2,1)S(1)} %bitcast.2, f32[8,512]{1,0:T(8,128)S(1)} %shard_map.28.own_ref), custom_call_target="tpu_custom_call" | custom-call | flops 1073741824 | bytes 8388608 | tf_op jit(solution)/shard_map/pallas_call | solution.py:339
  67.8 6.2 %shard_map.30 = f32[2,4096,512]{2,1,0:T(8,128)} custom-call(bf16[2,4096,512]{2,1,0:T(8,128)(2,1)S(1)} %bitcast.3, f32[4096,128]{1,0:T(8,128)S(1)} %get-tuple-element.9.weights_ref, bf16[2,384,512]{2,1,0:T(8,128)(2,1)S(1)} %get-tuple-element.10.panels_ref, f32[2,2560,512]{2,1,0:T(8,128)S(1)} %get-tuple-element.11.early_ref, ...), custom_call_target="tpu_custom_call" | custom-call | tf_op jit(solution)/shard_map/pallas_call | solution.py:411
Async XLA Ops:
  0.0 3.5 %copy-start = (bf16[8192,512]{1,0:T(8,128)(2,1)S(1)}, bf16[8192,512]{1,0:T(8,128)(2,1)}, u32[]{:S(2)}) copy-start(bf16[8192,512]{1,0:T(8,128)(2,1)} %emb_ref.1) | copy-start | bytes 25165828
  0.0 0.8 %copy-start.1 = (s32[2,32]{1,0:T(2,128)S(1)}, s32[2,32]{1,0:T(2,128)}, u32[]{:S(2)}) copy-start(s32[2,32]{1,0:T(2,128)} %picks_ref.1) | copy-start | bytes 772
